TPU v7x, 32 devices: a whole 2x2x4 slice. The times are simulated.
32 devices in a mesh: gx: 4 (over y, x), gy: 4 (over z), gz: 2 (over core).
Axes of the slice: x: 2, y: 2, z: 4, core: 2. Of those that a mesh axis runs over, the one named last changes fastest.
Arguments:
- tokens: bfloat16 [32, 8192, 128], P(('gx', 'gy', 'gz')), may hold values from -150 to 150
- task_id: int32 [32], P(('gx', 'gy', 'gz')), may hold values from 0 to 17
- valid_count: int32 [32], P(('gx', 'gy', 'gz')), may hold values from 2028 to 8115, as said below
- cross_params: bfloat16 [3029248], P(('gx', 'gy', 'gz')), may hold values from -50 to 50
- latent_params: bfloat16 [3150848], P(('gx', 'gy', 'gz')), may hold values from -50 to 50
- out_grad: bfloat16 [32, 512, 512], P(('gx', 'gy', 'gz')), may hold values from -6 to 6
Outputs:
- latents_out: bfloat16 [32, 512, 512], P(('gx', 'gy', 'gz'))
- token_grad: float32 [32, 8192, 128], P(('gx', 'gy', 'gz'))
- cross_grad: float32 [3029248], P(('gx', 'gy', 'gz'))
- latent_grad: float32 [3150848], P(('gx', 'gy', 'gz'))
Inputs may be any that keep to these rules, and one draw needn't show every extreme that they name: `valid_count`: patches at places below a scene's count are valid; some scene has all 8115 valid and some has 2028.
All inputs are finite; a program needn't handle non-finite values.
Results may differ from a plain program's by a relative error of at most 0.015.
Values may be sent and summed in bfloat16 or wider, within the bound.
No kernel may reach another device: no remote copies, remote signals or barrier semaphores. Data moves between devices by JAX's collectives and lax.ppermute only.
A program may use at most 256 MiB of HBM per device.

v0:
```python
import jax
import jax.numpy as jnp
from jax import lax
from jax.sharding import PartitionSpec as P

D = 512
FF = 2048
C = 128
LAT = 512
HEADS = 8
HEAD = 64
NTASK = 18
LANG = 77


epsilon = 1e-05
negative = -1e30


def cross_layout():
    return [
        ("latents", (LAT, D)),
        ("task_table", (NTASK, D)),
        ("query_gain", (D,)),
        ("query_bias", (D,)),
        ("context_gain", (C,)),
        ("context_bias", (C,)),
        ("query_weight", (D, D)),
        ("key_weight", (C, D)),
        ("value_weight", (C, D)),
        ("output_weight", (D, D)),
        ("output_bias", (D,)),
        ("feed_gain", (D,)),
        ("feed_bias", (D,)),
        ("up_weight", (D, FF)),
        ("up_bias", (FF,)),
        ("down_weight", (FF, D)),
        ("down_bias", (D,)),
    ]


def latent_layout():
    return [
        ("attend_gain", (D,)),
        ("attend_bias", (D,)),
        ("joint_weight", (D, 3 * D)),
        ("merge_weight", (D, D)),
        ("merge_bias", (D,)),
        ("feed_gain", (D,)),
        ("feed_bias", (D,)),
        ("up_weight", (D, FF)),
        ("up_bias", (FF,)),
        ("down_weight", (FF, D)),
        ("down_bias", (D,)),
    ]


def unpack(flat, layout):
    pieces = {}
    offset = 0
    for name, shape in layout:
        extent = 1
        for length in shape:
            extent = extent * length
        pieces[name] = flat[offset : offset + extent].reshape(shape)
        offset = offset + extent
    return pieces


def flatten(grads, layout, total_length):
    pieces = [grads[name].reshape(-1) for name, shape in layout]
    used = sum((piece.shape[0] for piece in pieces))
    pieces.append(jnp.zeros((total_length - used,), jnp.float32))
    return jnp.concatenate(pieces)


def layer_norm(value, gain, bias):
    centred = value - jnp.mean(value, axis=-1, keepdims=True)
    spread = jnp.mean(centred * centred, axis=-1, keepdims=True)
    return centred * lax.rsqrt(spread + epsilon) * gain + bias


def smooth(value):
    return jax.nn.gelu(value, approximate=False)


def widen(value):
    return value.astype(jnp.float32)


def narrow(value):
    return value.astype(jnp.bfloat16)


def product(left, right):
    return jnp.dot(left, right, preferred_element_type=jnp.float32)


def product_left(left, right):
    return lax.dot_general(
        left, right, (((0,), (0,)), ((), ())), preferred_element_type=jnp.float32
    )


def product_right(left, right):
    return lax.dot_general(
        left, right, (((1,), (1,)), ((), ())), preferred_element_type=jnp.float32
    )


def feed_forward(hidden, params):
    normed, norm_back = jax.vjp(
        layer_norm, hidden, widen(params["feed_gain"]), widen(params["feed_bias"])
    )
    normed_low = narrow(normed)
    inner = product(normed_low, params["up_weight"]) + widen(params["up_bias"])
    active, active_back = jax.vjp(smooth, inner)
    active_low = narrow(active)
    output = hidden + (product(active_low, params["down_weight"]) + widen(params["down_bias"]))
    return (output, (norm_back, normed_low, active_back, active_low))


def feed_backward(grad, saved, params):
    norm_back, normed_low, active_back, active_low = saved
    branch = narrow(grad)
    grads = {}
    grads["down_weight"] = product_left(active_low, branch)
    grads["down_bias"] = jnp.sum(widen(branch), axis=0)
    active_grad = product_right(branch, params["down_weight"])
    inner_low = narrow(active_back(active_grad)[0])
    grads["up_weight"] = product_left(normed_low, inner_low)
    grads["up_bias"] = jnp.sum(widen(inner_low), axis=0)
    normed_grad = product_right(inner_low, params["up_weight"])
    hidden_grad, grads["feed_gain"], grads["feed_bias"] = norm_back(normed_grad)
    return (grad + hidden_grad, grads)


def block_scores(query, keys, count, block, index):
    begin = index * block
    key_block = lax.dynamic_slice_in_dim(keys, begin, block, 0)
    raw = product_right(query, key_block) * D ** (-0.5)
    place = begin + jnp.arange(block, dtype=jnp.int32)
    valid = (place < count) | (place >= keys.shape[0] - LANG)
    return (jnp.where(valid[None, :], raw, negative), valid, begin)


def over_blocks(visit, init, blocks):

    def step(carry, index):
        return visit(carry, index)

    return lax.scan(step, init, jnp.arange(blocks, dtype=jnp.int32))


def cross_forward(scene, task, count, params, block):
    chosen = (jnp.arange(NTASK, dtype=jnp.int32) == task).astype(jnp.float32)
    start = widen(params["latents"]) + jnp.sum(
        chosen[:, None] * widen(params["task_table"]), axis=0
    )
    normed, norm_back = jax.vjp(
        layer_norm, start, widen(params["query_gain"]), widen(params["query_bias"])
    )
    normed_low = narrow(normed)
    context, context_back = jax.vjp(
        layer_norm, scene, widen(params["context_gain"]), widen(params["context_bias"])
    )
    context_low = narrow(context)
    query = narrow(product(normed_low, params["query_weight"]))
    keys = narrow(product(context_low, params["key_weight"]))
    values = narrow(product(context_low, params["value_weight"]))
    blocks = keys.shape[0] // block
    rows = query.shape[0]
    width = values.shape[1]

    def accumulate_total(carry, index):
        maxima, totals = carry
        scores, valid, begin = block_scores(query, keys, count, block, index)
        newest = jnp.maximum(maxima, jnp.max(scores, axis=-1))
        shifted = jnp.where(valid[None, :], jnp.exp(scores - newest[:, None]), 0.0)
        return ((newest, totals * jnp.exp(maxima - newest) + jnp.sum(shifted, axis=-1)), None)

    init = (jnp.full((rows,), negative, jnp.float32), jnp.zeros((rows,), jnp.float32))
    (maxima, totals), unused = over_blocks(accumulate_total, init, blocks)
    log_total = maxima + jnp.log(totals)

    def mix_values(total, index):
        scores, valid, begin = block_scores(query, keys, count, block, index)
        weights = narrow(jnp.where(valid[None, :], jnp.exp(scores - log_total[:, None]), 0.0))
        value_block = lax.dynamic_slice_in_dim(values, begin, block, 0)
        return (total + product(weights, value_block), None)

    mixed, unused = over_blocks(mix_values, jnp.zeros((rows, width), jnp.float32), blocks)
    mixed_low = narrow(mixed)
    after = start + (product(mixed_low, params["output_weight"]) + widen(params["output_bias"]))
    output, feed_saved = feed_forward(after, params)
    saved = (
        chosen,
        norm_back,
        normed_low,
        context_back,
        context_low,
        query,
        keys,
        values,
        log_total,
        mixed,
        mixed_low,
        feed_saved,
    )
    return (output, saved)


def cross_backward(grad, saved, params, count, block):
    (
        chosen,
        norm_back,
        normed_low,
        context_back,
        context_low,
        query,
        keys,
        values,
        log_total,
        mixed,
        mixed_low,
        feed_saved,
    ) = saved
    after_grad, grads = feed_backward(grad, feed_saved, params)
    branch = narrow(after_grad)
    grads["output_weight"] = product_left(mixed_low, branch)
    grads["output_bias"] = jnp.sum(widen(branch), axis=0)
    mixed_grad = narrow(product_right(branch, params["output_weight"]))
    blocks = keys.shape[0] // block
    rows = query.shape[0]
    width = values.shape[1]
    scale = D ** (-0.5)
    delta = jnp.sum(widen(mixed_grad) * mixed, axis=-1)

    def grad_pass(total, index):
        scores, valid, begin = block_scores(query, keys, count, block, index)
        weights = jnp.where(valid[None, :], jnp.exp(scores - log_total[:, None]), 0.0)
        value_block = lax.dynamic_slice_in_dim(values, begin, block, 0)
        key_block = lax.dynamic_slice_in_dim(keys, begin, block, 0)
        weights_grad = product_right(mixed_grad, value_block)
        scores_grad = narrow(weights * (weights_grad - delta[:, None]))
        keys_part = narrow(product_left(scores_grad, query) * scale)
        values_part = narrow(product_left(narrow(weights), mixed_grad))
        return (total + product(scores_grad, key_block), (keys_part, values_part))

    query_total, (keys_grad, values_grad) = over_blocks(
        grad_pass, jnp.zeros((rows, width), jnp.float32), blocks
    )
    query_grad = narrow(query_total * scale)
    keys_grad = keys_grad.reshape(blocks * block, width)
    values_grad = values_grad.reshape(blocks * block, width)
    grads["key_weight"] = product_left(context_low, keys_grad)
    grads["value_weight"] = product_left(context_low, values_grad)
    context_grad = product_right(keys_grad, params["key_weight"]) + product_right(
        values_grad, params["value_weight"]
    )
    token_grad, grads["context_gain"], grads["context_bias"] = context_back(context_grad)
    grads["query_weight"] = product_left(normed_low, query_grad)
    start_part, grads["query_gain"], grads["query_bias"] = norm_back(
        product_right(query_grad, params["query_weight"])
    )
    start_grad = after_grad + start_part
    grads["latents"] = start_grad
    grads["task_table"] = chosen[:, None] * jnp.sum(start_grad, axis=0)[None, :]
    return (token_grad, grads)


def latent_forward(hidden, params):
    normed, norm_back = jax.vjp(
        layer_norm, hidden, widen(params["attend_gain"]), widen(params["attend_bias"])
    )
    normed_low = narrow(normed)
    joint = narrow(product(normed_low, params["joint_weight"]))
    rows = hidden.shape[0]
    split = joint.reshape(rows, 3, HEADS, HEAD)
    query = split[:, 0]
    keys = split[:, 1]
    values = split[:, 2]
    scores = jnp.einsum("qhd,khd->hqk", query, keys, preferred_element_type=jnp.float32) * HEAD ** (
        -0.5
    )
    maxima = jnp.max(scores, axis=-1, keepdims=True)
    log_total = maxima + jnp.log(jnp.sum(jnp.exp(scores - maxima), axis=-1, keepdims=True))
    weights = narrow(jnp.exp(scores - log_total))
    mixed = jnp.einsum("hqk,khd->qhd", weights, values, preferred_element_type=jnp.float32).reshape(
        rows, HEADS * HEAD
    )
    mixed_low = narrow(mixed)
    after = hidden + (product(mixed_low, params["merge_weight"]) + widen(params["merge_bias"]))
    output, feed_saved = feed_forward(after, params)
    return (output, (norm_back, normed_low, query, keys, values, log_total, mixed_low, feed_saved))


def latent_backward(grad, saved, params):
    norm_back, normed_low, query, keys, values, log_total, mixed_low, feed_saved = saved
    after_grad, grads = feed_backward(grad, feed_saved, params)
    branch = narrow(after_grad)
    grads["merge_weight"] = product_left(mixed_low, branch)
    grads["merge_bias"] = jnp.sum(widen(branch), axis=0)
    rows = branch.shape[0]
    mixed_grad = narrow(product_right(branch, params["merge_weight"])).reshape(rows, HEADS, HEAD)
    scale = HEAD ** (-0.5)
    scores = jnp.einsum("qhd,khd->hqk", query, keys, preferred_element_type=jnp.float32) * scale
    weights = jnp.exp(scores - log_total)
    values_grad = jnp.einsum(
        "hqk,qhd->khd", narrow(weights), mixed_grad, preferred_element_type=jnp.float32
    )
    weights_grad = jnp.einsum(
        "qhd,khd->hqk", mixed_grad, values, preferred_element_type=jnp.float32
    )
    delta = jnp.sum(weights * weights_grad, axis=-1, keepdims=True)
    scores_grad = narrow(weights * (weights_grad - delta))
    query_grad = (
        jnp.einsum("hqk,khd->qhd", scores_grad, keys, preferred_element_type=jnp.float32) * scale
    )
    keys_grad = (
        jnp.einsum("hqk,qhd->khd", scores_grad, query, preferred_element_type=jnp.float32) * scale
    )
    joint_grad = narrow(
        jnp.stack([query_grad, keys_grad, values_grad], axis=1).reshape(rows, 3 * HEADS * HEAD)
    )
    grads["joint_weight"] = product_left(normed_low, joint_grad)
    hidden_grad, grads["attend_gain"], grads["attend_bias"] = norm_back(
        product_right(joint_grad, params["joint_weight"])
    )
    return (after_grad + hidden_grad, grads)


def body(tokens, task_id, valid_count, cross_params, latent_params, out_grad):
    cross_full = lax.all_gather(cross_params, ("gx", "gy", "gz"), axis=0, tiled=True)
    cross = unpack(cross_full, cross_layout())
    scene = widen(tokens[0])
    task = task_id[0]
    count = valid_count[0]
    block = min(1024, scene.shape[0])
    first, cross_saved = cross_forward(scene, task, count, cross, block)
    latent_full = lax.all_gather(latent_params, ("gx", "gy", "gz"), axis=0, tiled=True)
    latent = unpack(latent_full, latent_layout())
    result, latent_saved = latent_forward(first, latent)
    latents_out = narrow(result)[None]
    latent_back = unpack(
        lax.all_gather(latent_params, ("gx", "gy", "gz"), axis=0, tiled=True), latent_layout()
    )
    first_grad, latent_grads = latent_backward(widen(out_grad[0]), latent_saved, latent_back)
    latent_flat = flatten(latent_grads, latent_layout(), latent_full.shape[0])
    cross_back = unpack(
        lax.all_gather(cross_params, ("gx", "gy", "gz"), axis=0, tiled=True), cross_layout()
    )
    token_grad, cross_grads = cross_backward(first_grad, cross_saved, cross_back, count, block)
    cross_flat = flatten(cross_grads, cross_layout(), cross_full.shape[0])
    cross_share, latent_share = (
        lax.psum_scatter(cross_flat, ("gx", "gy", "gz"), scatter_dimension=0, tiled=True),
        lax.psum_scatter(latent_flat, ("gx", "gy", "gz"), scatter_dimension=0, tiled=True),
    )
    return (latents_out, token_grad[None], cross_share, latent_share)


def solution(mesh):
    return jax.shard_map(
        body,
        mesh=mesh,
        in_specs=(
            P(("gx", "gy", "gz"), None, None),
            P(("gx", "gy", "gz")),
            P(("gx", "gy", "gz")),
            P(("gx", "gy", "gz")),
            P(("gx", "gy", "gz")),
            P(("gx", "gy", "gz"), None, None),
        ),
        out_specs=(
            P(("gx", "gy", "gz"), None, None),
            P(("gx", "gy", "gz"), None, None),
            P(("gx", "gy", "gz")),
            P(("gx", "gy", "gz")),
        ),
        check_vma=False,
    )
```

profile of v0, /device:TPU:0, one launch (start us, length us, event | category | flops | bytes accessed | tf_op | source)
XLA Modules:
  0.0 1323.8 jit_solution(14570903620153120487)
XLA Ops:
  10.4 4.4 dynamic-update-slice.1
  27.1 227.2 %all-reduce.11.cloned.1.call-done = (bf16[3029248]{0:T(1024)(128)(2,1)}, bf16[3150848]{0:T(1024)(128)(2,1)}) async-done(((bf16[3029248]{0:T(1024)(128)(2,1)}, bf16[3150848]{0:T(1024)(128)(2,1)}), (bf16[3029248]{0:T(1024)(128)(2,1)}, bf16[3150848]{0:T(1024)(128)(2,1)})) %all-reduce.11.cloned.1.call-update) | async-done | bytes 12360208
  264.9 6.1 fusion.124
  288.2 6.1 convolution_convert_fusion.2
  294.3 60.8 %while.39 = (s32[]{:T(128)}, f32[512]{0:T(512)S(1)}, f32[512]{0:T(512)S(1)}, s32[8]{0:T(128)S(1)}, s32[]{:T(128)}, /*index=5*/bf16[8192,512]{1,0:T(8,128)(2,1)},...) while((s32[]{:T(128)}, f32[512]{0:T(512)S(1)}, ...), condition=%wide.region_8.9_spmd.clone, body=%wide.region_5.8_spmd.clone.sunk | while | flops 541071872 | bytes 5797054 | solution.py:152
  355.2 6.2 convolution_convert_fusion.1
  361.4 51.7 %while.40 = (s32[]{:T(128)}, f32[512,512]{1,0:T(8,128)}, s32[8]{0:T(128)S(1)}, s32[]{:T(128)}, bf16[8192,512]{1,0:T(8,128)(2,1)}, /*index=5*/bf16[512,512]{1,0:T...) while((s32[]{:T(128)}, f32[512,512]{1,0:T(8,128)}, ...), condition=%wide.region_10.11_spmd.clone, body=%wide.region_9.10_spmd.clone.sunk | while | flops 1076891648 | bytes 4724416 | solution.py:152
  369.8 4.5 convolution_add_fusion.9
  376.2 4.5 convolution_add_fusion.9
  382.7 4.5 convolution_add_fusion.9
  389.2 4.5 convolution_add_fusion.9
  395.6 4.5 convolution_add_fusion.9
  402.1 4.5 convolution_add_fusion.9
  408.6 4.5 convolution_add_fusion.9
  423.1 13.6 %multiply_convert_fusion.4 = (bf16[512,2048]{1,0:T(8,128)(2,1)S(1)}, f32[512,2048]{1,0:T(8,128)}, f32[512,2048]{1,0:T(8,128)}) fusion(f32[2048]{0:T(1024)S(1)} %get-tuple-element.448, bf16[512,2048]{1,0:T(8,128)(2,1)} %reshape.474, f32[512,512]{0,1:T(8,128)S(1)} %get-tuple-element.421, f32[512]{0:T(512)S(1)} %get-tuple-element.453, ...), kind=kOutput, calls=%fused_computation.101 | convolution fusion | flops 1144258560 | bytes 13647872 | tf_op jit(solution)/shard_map/dot_general | solution.py:96
  446.2 14.7 %copy.89 = bf16[512,1536]{0,1:T(8,128)(2,1)} copy(bf16[512,1536]{1,0:T(8,128)(2,1)} %convolution_convert_fusion.3) | data formatting | bytes 3145728 | tf_op jit(solution)/shard_map/convert_element_type | solution.py:92
  481.9 13.2 multiply_convert_fusion.3
  508.5 5.4 multiply_reduce_fusion
  535.8 5.1 convert_reduce_fusion.2
  554.6 103.4 %while.41 = (s32[]{:T(128)}, f32[512,512]{1,0:T(8,128)}, bf16[8,1024,512]{2,1,0:T(8,128)(2,1)}, bf16[8,1024,512]{2,1,0:T(8,128)(2,1)}, s32[8]{0:T(128)S(1)}, /*i...) while((s32[]{:T(128)}, f32[512,512]{1,0:T(8,128)}, ...), condition=%wide.region_28.29_spmd.clone, body=%wide.region_27.28_spmd.clone.sunk | while | flops 2690650112 | bytes 20978952 | solution.py:152
  664.4 7.9 fusion.135
  672.4 10.4 convolution_bitcast_fusion.9
  694.4 5.2 copy.129
  719.4 9.5 convolution_bitcast_fusion.8
  729.0 7.1 fusion.116
  749.8 36.6 %dynamic-update-slice.9 = f32[3150848]{0:T(1024)} dynamic-update-slice(f32[3150848]{0:T(1024)} %constant_dynamic-update-slice_fusion.18, f32[1048576]{0:T(1024)} %bitcast.249, s32[]{} %constant.197) | dynamic-update-slice | bytes 8388612
  787.8 36.5 %dynamic-update-slice.11 = f32[3150848]{0:T(1024)} dynamic-update-slice(f32[3150848]{0:T(1024)} %constant_dynamic-update-slice_fusion.17, f32[1048576]{0:T(1024)} %bitcast.247, s32[]{} %constant.199) | dynamic-update-slice | bytes 8388612
  828.8 7.5 fusion.47
  851.0 36.6 %dynamic-update-slice.26 = f32[3029248]{0:T(1024)} dynamic-update-slice(f32[3029248]{0:T(1024)} %constant_dynamic-update-slice_fusion.4, f32[1048576]{0:T(1024)} %bitcast.246, s32[]{} %constant.213) | dynamic-update-slice | bytes 8388612
  888.9 36.4 %dynamic-update-slice.28 = f32[3029248]{0:T(1024)} dynamic-update-slice(f32[3029248]{0:T(1024)} %constant_dynamic-update-slice_fusion.3, f32[1048576]{0:T(1024)} %bitcast.248, s32[]{} %constant.215) | dynamic-update-slice | bytes 8388612
  934.3 8.3 add_bitcast_fusion
  942.6 370.0 %all-reduce.9.cloned.1.call-done = (f32[3029248]{0:T(1024)}, f32[3150848]{0:T(1024)}) async-done(((f32[3029248]{0:T(1024)}, f32[3150848]{0:T(1024)}), (f32[3029248]{0:T(1024)}, f32[3150848]{0:T(1024)})) %all-reduce.9.cloned.1.call-update) | async-done | bytes 24720400
  (515 shorter events, 385.0 us)
Async XLA Ops:
  7.2 247.1 %all-reduce.11.cloned.1.call-start = ((), (), s32[]{:S(2)}) async-start(), calls=%async_computation.1 | async-start | bytes 24723456
  21.4 1291.3 %all-reduce.9.cloned.1.call-start = ((), (), s32[]{:S(2)}) async-start(), calls=%async_computation | async-start | bytes 49446912
  23.4 236.9 %copy-start.88 = (f32[18]{0:T(128)}, f32[18]{0:T(128)S(1)}, u32[]{:S(2)}) copy-start(f32[18]{0:T(128)S(1)} %compare_convert_fusion) | copy-start | bytes 220
  24.1 331.1 %copy-start.38 = (f32[8192]{0:T(1024)}, f32[8192]{0:T(1024)S(1)}, u32[]{:S(2)}) copy-start(f32[8192]{0:T(1024)S(1)} %broadcast_multiply_fusion.1) | copy-start | bytes 98308
  27.1 328.1 %copy-start.50 = (f32[8192]{0:T(1024)}, f32[8192]{0:T(1024)S(1)}, u32[]{:S(2)}) copy-start(f32[8192]{0:T(1024)S(1)} %fusion.92) | copy-start | bytes 98308
  260.3 153.2 %copy-start.3 = (f32[512,512]{0,1:T(8,128)}, f32[512,512]{0,1:T(8,128)S(1)}, u32[]{:S(2)}) copy-start(f32[512,512]{0,1:T(8,128)S(1)} %copy.83) | copy-start | bytes 3145732
  260.4 153.0 %copy-start.66 = (f32[512]{0:T(512)}, f32[512]{0:T(512)S(1)}, u32[]{:S(2)}) copy-start(f32[512]{0:T(512)S(1)} %multiply_reduce_fusion.15) | copy-start | bytes 6148
  260.8 15.5 %copy-start.76 = (f32[512]{0:T(512)}, f32[512]{0:T(512)S(1)}, u32[]{:S(2)}) copy-start(f32[512]{0:T(512)S(1)} %multiply_reduce_fusion.14) | copy-start | bytes 6148
  261.8 93.3 %copy-start.74 = (f32[128]{0:T(128)}, f32[128]{0:T(128)S(1)}, u32[]{:S(2)}) copy-start(f32[128]{0:T(128)S(1)} %get-tuple-element.417) | copy-start | bytes 1540
  261.8 93.4 %copy-start.80 = (f32[128]{0:T(128)}, f32[128]{0:T(128)S(1)}, u32[]{:S(2)}) copy-start(f32[128]{0:T(128)S(1)} %get-tuple-element.418) | copy-start | bytes 1540
  264.9 12.1 copy-start.70
  264.9 12.5 copy-start.78
  361.4 51.7 %copy-start.40 = (bf16[262144]{0:T(1024)(128)(2,1)S(1)}, bf16[262144]{0:T(1024)(128)(2,1)}, u32[]{:S(2)}) copy-start(bf16[262144]{0:T(1024)(128)(2,1)} %get-tuple-element.415) | copy-start | bytes 1572868
  423.1 13.6 %copy-start.43 = (bf16[2048,512]{1,0:T(8,128)(2,1)S(1)}, bf16[2048,512]{1,0:T(8,128)(2,1)}, u32[]{:S(2)}) copy-start(bf16[2048,512]{1,0:T(8,128)(2,1)} %reshape.475) | copy-start | bytes 6291460
  473.0 54.7 %copy-start.6 = (f32[512,512]{0,1:T(8,128)}, f32[512,512]{0,1:T(8,128)S(1)}, u32[]{:S(2)}) copy-start(f32[512,512]{0,1:T(8,128)S(1)} %get-tuple-element.428) | copy-start | bytes 3145732
  481.9 13.2 copy-start.41
  481.9 13.2 copy-start.59
  554.5 103.5 %copy-start.4 = (f32[512,512]{0,1:T(8,128)S(1)}, f32[512,512]{0,1:T(8,128)}, u32[]{:S(2)}) copy-start(f32[512,512]{0,1:T(8,128)} %copy-done.3) | copy-start | bytes 3145732
  554.5 103.5 %copy-start.67 = (f32[512]{0:T(512)S(1)}, f32[512]{0:T(512)}, u32[]{:S(2)}) copy-start(f32[512]{0:T(512)} %copy-done.66) | copy-start | bytes 6148
  554.6 103.5 %copy-start.69 = (f32[512]{0:T(512)S(1)}, f32[512]{0:T(512)}, u32[]{:S(2)}) copy-start(f32[512]{0:T(512)} %copy-done.68) | copy-start | bytes 6148
  554.6 103.5 %copy-start.71 = (f32[512]{0:T(512)S(1)}, f32[512]{0:T(512)}, u32[]{:S(2)}) copy-start(f32[512]{0:T(512)} %copy-done.70) | copy-start | bytes 6148
  554.6 103.5 %copy-start.73 = (f32[512]{0:T(512)S(1)}, f32[512]{0:T(512)}, u32[]{:S(2)}) copy-start(f32[512]{0:T(512)} %copy-done.72) | copy-start | bytes 6148
  554.6 103.5 %copy-start.79 = (f32[512]{0:T(512)S(1)}, f32[512]{0:T(512)}, u32[]{:S(2)}) copy-start(f32[512]{0:T(512)} %copy-done.78) | copy-start | bytes 6148
  672.4 11.9 copy-start.14
  672.4 11.9 copy-start.96
  787.8 36.5 %copy-start.83 = (f32[512]{0:T(512)S(1)}, f32[512]{0:T(512)}, u32[]{:S(2)}) copy-start(f32[512]{0:T(512)} %get-tuple-element.419) | copy-start | bytes 6148
  824.3 13.4 %copy-start.94 = (f32[128]{0:T(128)S(1)}, f32[128]{0:T(128)}, u32[]{:S(2)}) copy-start(f32[128]{0:T(128)} %get-tuple-element.310) | copy-start | bytes 1540
  824.3 14.7 %copy-start.33 = (f32[64,4,8,128]{3,1,2,0:T(4,128)S(1)}, f32[64,4,8,128]{3,1,2,0:T(4,128)}, u32[]{:S(2)}) copy-start(f32[64,4,8,128]{3,1,2,0:T(4,128)} %copy.122) | copy-start | bytes 3145732
  828.8 12.5 copy-start.56
  836.4 12.0 copy-start.82
  836.4 13.3 %copy-start.92 = (f32[512]{0:T(512)S(1)}, f32[512]{0:T(512)}, u32[]{:S(2)}) copy-start(f32[512]{0:T(512)} %get-tuple-element.437) | copy-start | bytes 6148
  851.0 36.6 %copy-start.85 = (f32[2048]{0:T(1024)S(1)}, f32[2048]{0:T(1024)}, u32[]{:S(2)}) copy-start(f32[2048]{0:T(1024)} %get-tuple-element.439) | copy-start | bytes 24580
  (78 other events, 366.3 us)
Sparse Core Ops, SparseCore 0:
  21.5 232.6 all-reduce.10
  926.8 385.8 all-reduce.8
where the time goes:
time: 1350 us; the launch traced here: 1320 us
  waiting for transfers between devices  597 us (44%)
  local copies, waits for them, and re-layouts  316 us (23%)
  matrix products  296 us (22%)
  other arithmetic  81.5 us (6%)
  between operations  16.5 us (1%)
  loops' own time  16.3 us (1%)
    unnamed x4, waiting for transfers between devices  597 us
    unnamed x255, local copies, waits for them, and re-layouts  226 us
    dot_general x26, matrix products, product(): return jnp.dot(left, right, preferred_element_type=jnp.float32)  116 us
    dot_general x34, matrix products, product_right(): lax.dot_general(left, right, (((1,), (1,)), ((), ())), preferred_element_...  98.5 us
    dot_general x26, matrix products, product_left(): lax.dot_general(left, right, (((0,), (0,)), ((), ())), preferred_element_...  66.7 us
  transfers between devices with their start and end apart: 2, of which 2 were waited for; matrix products, arithmetic and copies ran while one was open for 1% of the time, Pallas kernels for 0%

commit v1 on v0

v1 whole, which is shorter than its diff:
```python
import functools
import math
import types

import jax
import jax.numpy as jnp
from jax import lax
from jax.experimental import pallas as pl
from jax.experimental.pallas import tpu as pltpu
from jax.sharding import PartitionSpec as P

D = 512
FF = 2048
C = 128
LAT = 512
HEADS = 8
HEAD = 64
NTASK = 18
LANG = 77
LANES = 128
TILE = 16
UNIT = TILE * LANES
BLOCK = 1024
AXES = ("gx", "gy", "gz")

epsilon = 1e-05
negative = -1e30
LOG2E = math.log2(math.e)
bf16 = jnp.bfloat16
f32 = jnp.float32
VMEM_LIMIT = 60 * 1024 * 1024


def layout_of(**shapes):
    table = {}
    row = 0
    for name, dims in shapes.items():
        table[name] = (row, dims)
        row += math.prod(dims) // LANES
    return types.SimpleNamespace(**table), row


CROSS, CROSS_ROWS = layout_of(
    latents=(LAT, D),
    task_table=(NTASK, D),
    query_gain=(D,),
    query_bias=(D,),
    context_gain=(C,),
    context_bias=(C,),
    query_weight=(D, D),
    key_weight=(C, D),
    value_weight=(C, D),
    output_weight=(D, D),
    output_bias=(D,),
    feed_gain=(D,),
    feed_bias=(D,),
    up_weight=(D, FF),
    up_bias=(FF,),
    down_weight=(FF, D),
    down_bias=(D,),
)
LATENT, LATENT_ROWS = layout_of(
    attend_gain=(D,),
    attend_bias=(D,),
    joint_weight=(D, 3 * D),
    merge_weight=(D, D),
    merge_bias=(D,),
    feed_gain=(D,),
    feed_bias=(D,),
    up_weight=(D, FF),
    up_bias=(FF,),
    down_weight=(FF, D),
    down_bias=(D,),
)


def vectors_of(table):
    return [place for place in vars(table).values() if len(place[1]) == 1]


class Windows:
    def __init__(self, total, devices):
        self.total = total
        self.devices = devices
        self.shard = total // devices
        starts = [self.shard * d for d in range(devices)]
        self.first = [s // UNIT * TILE for s in starts]
        self.phase = [s % UNIT for s in starts]
        self.rows = max(-(-(p + self.shard) // UNIT) * TILE for p in self.phase)
        self.padded = max(f + self.rows for f in self.first)
        self.full = -(-total // UNIT) * TILE
        self.shard_rows = -(-self.shard // (8 * LANES)) * 8


def dot(left, right):
    return jnp.dot(left, right, preferred_element_type=f32)


def dot_nt(left, right):
    return lax.dot_general(left, right, (((1,), (1,)), ((), ())), preferred_element_type=f32)


def dot_tn(left, right):
    return lax.dot_general(left, right, (((0,), (0,)), ((), ())), preferred_element_type=f32)


def split(value, axis):
    high = value.astype(bf16)
    low = (value - high.astype(f32)).astype(bf16)
    return jnp.concatenate([high, low], axis=axis)


def normalise(value):
    centred = value - jnp.mean(value, axis=-1, keepdims=True)
    rstd = lax.rsqrt(jnp.mean(centred * centred, axis=-1, keepdims=True) + epsilon)
    return centred * rstd, rstd


def normalise_back(grad, unit, rstd, gain):
    inner = grad * gain
    return rstd * (
        inner
        - jnp.mean(inner, axis=-1, keepdims=True)
        - unit * jnp.mean(inner * unit, axis=-1, keepdims=True)
    )


def column_sum(value):
    return jnp.sum(value, axis=0, keepdims=True)


def vmem_specs(count):
    return [pl.BlockSpec(memory_space=pltpu.VMEM)] * count


def shape(dims, dtype):
    return jax.ShapeDtypeStruct(dims, dtype)


def call(kernel, name, outs, inputs, scratch=(), smem=0, flops=0, moved=0):
    specs = [pl.BlockSpec(memory_space=pltpu.SMEM)] * smem + vmem_specs(len(inputs) - smem)
    return pl.pallas_call(
        kernel,
        name=name,
        out_shape=outs,
        in_specs=specs,
        out_specs=jax.tree.map(lambda _: pl.BlockSpec(memory_space=pltpu.VMEM), outs),
        scratch_shapes=list(scratch),
        compiler_params=pltpu.CompilerParams(vmem_limit_bytes=VMEM_LIMIT),
        cost_estimate=pl.CostEstimate(flops=flops, bytes_accessed=moved, transcendentals=0),
    )(*inputs)


def place_kernel(shift_ref, shard_ref, out_ref):
    rows = shard_ref.shape[0]
    down, across = shift_ref[0] // LANES, shift_ref[0] % LANES
    value = shard_ref[...].astype(f32)
    turned = pltpu.roll(value, across, axis=1)
    above = pltpu.roll(turned, 1, axis=0)
    lane = lax.broadcasted_iota(jnp.int32, (rows, LANES), 1)
    out_ref[...] = pltpu.roll(jnp.where(lane < across, above, turned), down, axis=0).astype(bf16)


def place(shard, windows, index):
    rows = windows.rows
    padded = jnp.pad(shard, (0, rows * LANES - windows.shard)).reshape(rows, LANES)
    shift = (windows.shard * index) % UNIT
    return call(place_kernel, "place", shape((rows, LANES), bf16), [shift.reshape(1), padded], smem=1)


def extract_kernel(shift_ref, window_ref, out_ref):
    rows = window_ref.shape[0]
    down, across = shift_ref[0] // LANES, shift_ref[0] % LANES
    value = window_ref[...].astype(f32)
    turned = pltpu.roll(value, lax.rem(LANES - across, LANES), axis=1)
    below = pltpu.roll(turned, rows - 1, axis=0)
    lane = lax.broadcasted_iota(jnp.int32, (rows, LANES), 1)
    merged = pltpu.roll(
        jnp.where(lane < LANES - across, turned, below), lax.rem(rows - down, rows), axis=0
    )
    out_ref[...] = merged[: out_ref.shape[0]]


def extract(window, windows, index):
    shift = (windows.shard * index) % UNIT
    rows = min(windows.shard_rows, windows.rows)
    found = call(
        extract_kernel, "extract", shape((rows, LANES), f32), [shift.reshape(1), window], smem=1
    )
    return found.reshape(-1)[: windows.shard]


def assemble(gathered_ref, flat_ref, windows):
    rows = windows.rows
    for d in range(windows.devices):
        first = windows.first[d]
        last = windows.first[d + 1] if d + 1 < windows.devices else windows.full - TILE
        block = gathered_ref[d * rows : d * rows + last + TILE - first, :].astype(f32)
        if windows.phase[d]:
            flat_ref[first : first + TILE, :] += block[:TILE]
            flat_ref[first + TILE : last + TILE, :] = block[TILE:]
        else:
            flat_ref[first : last + TILE, :] = block


def relay(flat_ref, place, out_ref):
    first, (rows, columns) = place
    chunks = columns // LANES
    step = 64

    def body(index, carry):
        begin = pl.multiple_of(index * step, step)
        for chunk in range(chunks):
            part = flat_ref[pl.ds(first + begin * chunks + chunk, step, stride=chunks), :]
            out_ref[pl.ds(begin, step), chunk * LANES : (chunk + 1) * LANES] = part.astype(out_ref.dtype)
        return carry

    lax.fori_loop(0, rows // step, body, 0)


def relay_vectors(flat_ref, table, out_ref):
    for index, (first, dims) in enumerate(vectors_of(table)):
        for chunk in range(dims[0] // LANES):
            out_ref[index : index + 1, chunk * LANES : (chunk + 1) * LANES] = flat_ref[
                first + chunk : first + chunk + 1, :
            ]


def unpack_cross_kernel(windows, task_ref, gathered_ref, vectors_ref, start_ref, query_ref, key_ref,
                        value_ref, output_ref, up_ref, down_ref, flat_ref):
    assemble(gathered_ref, flat_ref, windows)
    relay_vectors(flat_ref, CROSS, vectors_ref)
    chunks = D // LANES
    first, unused = CROSS.task_table
    base = first + task_ref[0] * chunks
    relay(flat_ref, CROSS.latents, start_ref)
    for chunk in range(chunks):
        row = flat_ref[pl.ds(base + chunk, 1), :]
        start_ref[:, chunk * LANES : (chunk + 1) * LANES] += row
    relay(flat_ref, CROSS.query_weight, query_ref)
    relay(flat_ref, CROSS.key_weight, key_ref)
    relay(flat_ref, CROSS.value_weight, value_ref)
    relay(flat_ref, CROSS.output_weight, output_ref)
    relay(flat_ref, CROSS.up_weight, up_ref)
    relay(flat_ref, CROSS.down_weight, down_ref)


def unpack_cross(gathered, task, windows):
    outs = [
        shape((16, FF), f32), shape((LAT, D), f32), shape((D, D), bf16), shape((C, D), bf16),
        shape((C, D), bf16), shape((D, D), bf16), shape((D, FF), bf16), shape((FF, D), bf16),
    ]
    return call(
        functools.partial(unpack_cross_kernel, windows), "unpack_cross", outs, [task, gathered],
        scratch=[pltpu.VMEM((windows.full, LANES), f32)], smem=1,
    )


def unpack_latent_kernel(windows, gathered_ref, vectors_ref, joint_ref, merge_ref, up_ref, down_ref,
                         flat_ref):
    assemble(gathered_ref, flat_ref, windows)
    relay_vectors(flat_ref, LATENT, vectors_ref)
    relay(flat_ref, LATENT.joint_weight, joint_ref)
    relay(flat_ref, LATENT.merge_weight, merge_ref)
    relay(flat_ref, LATENT.up_weight, up_ref)
    relay(flat_ref, LATENT.down_weight, down_ref)


def unpack_latent(gathered, windows):
    outs = [
        shape((8, FF), f32), shape((D, 3 * D), bf16), shape((D, D), bf16), shape((D, FF), bf16),
        shape((FF, D), bf16),
    ]
    return call(
        functools.partial(unpack_latent_kernel, windows), "unpack_latent", outs, [gathered],
        scratch=[pltpu.VMEM((windows.full, LANES), f32)],
    )


def put(flat_ref, first, columns, row, value, column=0):
    chunks = columns // LANES
    rows = value.shape[0]
    for chunk in range(value.shape[1] // LANES):
        begin = first + row * chunks + column // LANES + chunk
        flat_ref[pl.ds(begin, rows, stride=chunks), :] = value[:, chunk * LANES : (chunk + 1) * LANES]


def put_vector(flat_ref, first, value, column=0):
    for chunk in range(value.shape[1] // LANES):
        row = first + column // LANES + chunk
        flat_ref[row : row + 1, :] = value[:, chunk * LANES : (chunk + 1) * LANES]


def to_windows(flat_ref, out_ref, windows):
    rows = windows.rows
    for d in range(windows.devices):
        first = windows.first[d]
        out_ref[d * rows : (d + 1) * rows, :] = flat_ref[first : first + rows, :].astype(bf16)


def clear_tail(flat_ref, used):
    total = flat_ref.shape[0]
    flat_ref[used:total, :] = jnp.zeros((total - used, LANES), f32)


def gelu_and_slope(value):
    half = 0.5 + 0.5 * lax.erf(value * math.sqrt(0.5))
    density = jnp.exp2(value * value * (-0.5 * LOG2E)) * (1.0 / math.sqrt(2.0 * math.pi))
    return value * half, half + value * density


def feed_forward(hidden, gain, bias, up_ref, up_bias, down_ref, down_bias, normed_ref, active_ref, slope_ref):
    unit, rstd = normalise(hidden)
    normed_ref[...] = (unit * gain + bias).astype(bf16)
    step = 256
    for begin in range(0, FF, step):
        inner = dot(normed_ref[...], up_ref[:, begin : begin + step]) + up_bias[:, begin : begin + step]
        active, slope = gelu_and_slope(inner)
        active_ref[:, begin : begin + step] = active.astype(bf16)
        slope_ref[:, begin : begin + step] = slope.astype(bf16)
    return hidden + (dot(active_ref[...], down_ref[...]) + down_bias)


def feed_backward(grad, hidden, gain, up_ref, down_ref, normed_ref, active_ref, slope_ref, flat_ref, table):
    unit, rstd = normalise(hidden)
    branch = grad.astype(bf16)
    put_vector(flat_ref, table.down_bias[0], column_sum(branch.astype(f32)))
    step = 256
    total = None
    normed = normed_ref[...]
    for begin in range(0, FF, step):
        put(flat_ref, table.down_weight[0], D, begin, dot_tn(active_ref[:, begin : begin + step], branch))
        active_grad = dot_nt(branch, down_ref[begin : begin + step, :])
        inner = (active_grad * slope_ref[:, begin : begin + step].astype(f32)).astype(bf16)
        slope_ref[:, begin : begin + step] = inner
        put_vector(flat_ref, table.up_bias[0], column_sum(inner.astype(f32)), begin)
        put(flat_ref, table.up_weight[0], FF, 0, dot_tn(normed, inner), begin)
    normed_grad = dot_nt(slope_ref[...], up_ref[...])
    put_vector(flat_ref, table.feed_gain[0], column_sum(normed_grad * unit))
    put_vector(flat_ref, table.feed_bias[0], column_sum(normed_grad))
    return grad + normalise_back(normed_grad, unit, rstd, gain)


def vector(vectors_ref, table, place):
    index = vectors_of(table).index(place)
    return vectors_ref[index : index + 1, : place[1][0]]


def block_kinds(count, begin, block, total):
    language = total - LANG
    end = begin + block
    some = (begin < count) | (end > language)
    full = (end <= count) | (count >= language) | (begin >= language)
    return some, full


def masked(scores, count, begin, total):
    place = begin + lax.broadcasted_iota(jnp.int32, (scores.shape[0], 1), 0)
    valid = (place < count) | (place >= total - LANG)
    return jnp.where(valid, scores, negative)


def cross_forward_kernel(count_ref, tokens_ref, start_ref, vectors_ref, wq_ref, wk_ref, wv_ref, wo_ref,
                         up_ref, down_ref,
                         normedq_ref, query_ref, keyed_ref, mixture_ref, lse_ref, hidden_ref, normed_ref,
                         active_ref, slope_ref, out_ref,
                         scores_ref, acc_ref, max_ref, sum_ref):
    total = tokens_ref.shape[0]
    count = count_ref[0]
    start = start_ref[...]
    unit, rstd = normalise(start)
    normedq_ref[...] = (
        unit * vector(vectors_ref, CROSS, CROSS.query_gain) + vector(vectors_ref, CROSS, CROSS.query_bias)
    ).astype(bf16)
    query_ref[...] = dot(normedq_ref[...], wq_ref[...]).astype(bf16)
    keyed_ref[...] = dot_nt(query_ref[...], wk_ref[...]) * D ** (-0.5)
    keyed = split(keyed_ref[...] * LOG2E, 1)
    gain = vector(vectors_ref, CROSS, CROSS.context_gain)
    bias = vector(vectors_ref, CROSS, CROSS.context_bias)
    max_ref[...] = jnp.full(max_ref.shape, negative, f32)
    sum_ref[...] = jnp.zeros(sum_ref.shape, f32)
    acc_ref[...] = jnp.zeros(acc_ref.shape, f32)
    block = scores_ref.shape[0]

    def visit(index, carry):
        begin = pl.multiple_of(index * block, block)
        some, full = block_kinds(count, begin, block, total)

        @pl.when(some)
        def _():
            unit, rstd = normalise(tokens_ref[pl.ds(begin, block), :].astype(f32))
            context = (unit * gain + bias).astype(bf16)
            scores_ref[...] = dot_nt(jnp.concatenate([context, context], axis=1), keyed)

            @pl.when(jnp.logical_not(full))
            def _():
                scores_ref[...] = masked(scores_ref[...], count, begin, total)

            old = max_ref[...]
            newest = jnp.maximum(old, jnp.max(scores_ref[...], axis=0, keepdims=True))
            weights = jnp.exp2(scores_ref[...] - newest)
            fade = jnp.exp2(old - newest)
            max_ref[...] = newest
            sum_ref[...] = sum_ref[...] * fade + column_sum(weights)
            acc_ref[...] = acc_ref[...] * fade + dot_tn(context, weights.astype(bf16))

        return carry

    lax.fori_loop(0, total // block, visit, 0)
    totals = sum_ref[...]
    lse_ref[...] = max_ref[...] + jnp.log2(totals)
    mixture_ref[...] = acc_ref[...] * (1.0 / totals)
    values = jnp.concatenate([wv_ref[...], wv_ref[...]], axis=0)
    attended = dot_tn(split(mixture_ref[...], 0), values)
    hidden_ref[...] = start + (
        dot(attended.astype(bf16), wo_ref[...]) + vector(vectors_ref, CROSS, CROSS.output_bias)
    )
    out_ref[...] = feed_forward(
        hidden_ref[...], vector(vectors_ref, CROSS, CROSS.feed_gain), vector(vectors_ref, CROSS, CROSS.feed_bias),
        up_ref, vector(vectors_ref, CROSS, CROSS.up_bias), down_ref, vector(vectors_ref, CROSS, CROSS.down_bias),
        normed_ref, active_ref, slope_ref,
    )


def cross_forward(count, tokens, start, vectors, wq, wk, wv, wo, up, down):
    block = min(BLOCK, tokens.shape[0])
    outs = [
        shape((LAT, D), bf16), shape((LAT, D), bf16), shape((LAT, C), f32), shape((C, LAT), f32),
        shape((1, LAT), f32), shape((LAT, D), f32), shape((LAT, D), bf16), shape((LAT, FF), bf16),
        shape((LAT, FF), bf16), shape((LAT, D), f32),
    ]
    scratch = [
        pltpu.VMEM((block, LAT), f32), pltpu.VMEM((C, LAT), f32), pltpu.VMEM((1, LAT), f32),
        pltpu.VMEM((1, LAT), f32),
    ]
    return call(
        cross_forward_kernel, "cross_forward", outs,
        [count, tokens, start, vectors, wq, wk, wv, wo, up, down], scratch=scratch, smem=1,
        flops=15_000_000_000, moved=16_000_000,
    )


def pair_mask(value, side):
    lane = lax.broadcasted_iota(jnp.int32, (1, LANES), 1)
    keep = (lane < HEAD) if side == 0 else (lane >= HEAD)
    return jnp.where(keep, value, jnp.zeros_like(value))


def latent_kernel(windows, hidden_ref, cotangent_ref, vectors_ref, joint_w_ref, merge_ref, up_ref, down_ref,
                  out_ref, grad_ref, windows_ref,
                  flat_ref, probs_ref, joint_ref, mixed_ref, after_ref, normedl_ref, normed_ref, active_ref,
                  slope_ref, query_grad_ref, joint_grad_ref):
    gain = vector(vectors_ref, LATENT, LATENT.attend_gain)
    unit, rstd = normalise(hidden_ref[...])
    normedl_ref[...] = (unit * gain + vector(vectors_ref, LATENT, LATENT.attend_bias)).astype(bf16)
    joint_ref[...] = dot(normedl_ref[...], joint_w_ref[...]).astype(bf16)
    scale = HEAD ** (-0.5)
    for pair in range(HEADS // 2):
        lanes = slice(pair * LANES, (pair + 1) * LANES)
        query = joint_ref[:, lanes]
        keys = joint_ref[:, D + pair * LANES : D + (pair + 1) * LANES]
        values = joint_ref[:, 2 * D + pair * LANES : 2 * D + (pair + 1) * LANES]
        mixed = None
        for side in range(2):
            scores = dot_nt(pair_mask(keys, side), query) * (scale * LOG2E)
            weights = jnp.exp2(scores - jnp.max(scores, axis=0, keepdims=True))
            weights = weights * (1.0 / column_sum(weights))
            probs_ref[2 * pair + side] = weights
            part = dot_tn(pair_mask(values, side), weights.astype(bf16))
            mixed = part if mixed is None else mixed + part
        mixed_ref[lanes, :] = mixed.astype(bf16)
    after_ref[...] = hidden_ref[...] + (
        dot_tn(mixed_ref[...], merge_ref[...]) + vector(vectors_ref, LATENT, LATENT.merge_bias)
    )
    feed_gain = vector(vectors_ref, LATENT, LATENT.feed_gain)
    out_ref[...] = feed_forward(
        after_ref[...], feed_gain, vector(vectors_ref, LATENT, LATENT.feed_bias), up_ref,
        vector(vectors_ref, LATENT, LATENT.up_bias), down_ref, vector(vectors_ref, LATENT, LATENT.down_bias),
        normed_ref, active_ref, slope_ref,
    ).astype(bf16)

    clear_tail(flat_ref, LATENT_ROWS)
    after_grad = feed_backward(
        cotangent_ref[...].astype(f32), after_ref[...], feed_gain, up_ref, down_ref, normed_ref, active_ref,
        slope_ref, flat_ref, LATENT,
    )
    branch = after_grad.astype(bf16)
    put(flat_ref, LATENT.merge_weight[0], D, 0, dot(mixed_ref[...], branch))
    put_vector(flat_ref, LATENT.merge_bias[0], column_sum(branch.astype(f32)))
    mixed_grad = dot_nt(branch, merge_ref[...]).astype(bf16)
    for pair in range(HEADS // 2):
        lanes = slice(pair * LANES, (pair + 1) * LANES)
        query = joint_ref[:, lanes]
        keys = joint_ref[:, D + pair * LANES : D + (pair + 1) * LANES]
        values = joint_ref[:, 2 * D + pair * LANES : 2 * D + (pair + 1) * LANES]
        grads = mixed_grad[:, lanes]
        query_part = key_part = value_part = None
        for side in range(2):
            probs = probs_ref[2 * pair + side]
            part = dot(probs.astype(bf16), pair_mask(grads, side))
            value_part = part if side == 0 else value_part + part
            probs_grad = dot_nt(pair_mask(values, side), grads)
            delta = column_sum(probs * probs_grad)
            scores_grad = (probs * (probs_grad - delta)).astype(bf16)
            part = dot(scores_grad, pair_mask(query, side))
            key_part = part if side == 0 else key_part + part
            part = dot_tn(pair_mask(keys, side), scores_grad)
            query_part = part if side == 0 else query_part + part
        query_grad_ref[lanes, :] = query_part * scale
        joint_grad_ref[:, D + pair * LANES : D + (pair + 1) * LANES] = (key_part * scale).astype(bf16)
        joint_grad_ref[:, 2 * D + pair * LANES : 2 * D + (pair + 1) * LANES] = value_part.astype(bf16)
    joint_grad_ref[:, :D] = query_grad_ref[...].T.astype(bf16)
    put(flat_ref, LATENT.joint_weight[0], 3 * D, 0, dot_tn(normedl_ref[...], joint_grad_ref[...]))
    normed_grad = dot_nt(joint_grad_ref[...], joint_w_ref[...])
    put_vector(flat_ref, LATENT.attend_gain[0], column_sum(normed_grad * unit))
    put_vector(flat_ref, LATENT.attend_bias[0], column_sum(normed_grad))
    grad_ref[...] = after_grad + normalise_back(normed_grad, unit, rstd, gain)
    to_windows(flat_ref, windows_ref, windows)


def latent_layer(hidden, cotangent, vectors, joint, merge, up, down, windows):
    outs = [
        shape((LAT, D), bf16), shape((LAT, D), f32),
        shape((windows.devices * windows.rows, LANES), bf16),
    ]
    scratch = [
        pltpu.VMEM((windows.padded, LANES), f32), pltpu.VMEM((HEADS, LAT, LAT), f32),
        pltpu.VMEM((LAT, 3 * D), bf16), pltpu.VMEM((D, LAT), bf16), pltpu.VMEM((LAT, D), f32),
        pltpu.VMEM((LAT, D), bf16), pltpu.VMEM((LAT, D), bf16), pltpu.VMEM((LAT, FF), bf16),
        pltpu.VMEM((LAT, FF), bf16), pltpu.VMEM((D, LAT), f32), pltpu.VMEM((LAT, 3 * D), bf16),
    ]
    return call(
        functools.partial(latent_kernel, windows), "latent_layer", outs,
        [hidden, cotangent, vectors, joint, merge, up, down], scratch=scratch,
        flops=20_000_000_000, moved=16_000_000,
    )


def cross_backward_kernel(windows, count_ref, task_ref, tokens_ref, grad_ref, start_ref, vectors_ref, wq_ref,
                          wk_ref, wv_ref, wo_ref, up_ref, down_ref, normedq_ref, query_ref, keyed_ref,
                          mixture_ref, lse_ref, hidden_ref, normed_ref, active_ref, saved_slope_ref,
                          token_grad_ref, windows_ref,
                          flat_ref, slope_ref, scores_ref, acc_ref, gains_ref):
    total = tokens_ref.shape[0]
    count = count_ref[0]
    clear_tail(flat_ref, CROSS_ROWS)
    slope_ref[...] = saved_slope_ref[...]
    hidden_grad = feed_backward(
        grad_ref[...], hidden_ref[...], vector(vectors_ref, CROSS, CROSS.feed_gain), up_ref, down_ref, normed_ref,
        active_ref, slope_ref, flat_ref, CROSS,
    )
    branch = hidden_grad.astype(bf16)
    values = jnp.concatenate([wv_ref[...], wv_ref[...]], axis=0)
    mixture = split(mixture_ref[...], 0)
    attended = dot_tn(mixture, values)
    put(flat_ref, CROSS.output_weight[0], D, 0, dot_tn(attended.astype(bf16), branch))
    put_vector(flat_ref, CROSS.output_bias[0], column_sum(branch.astype(f32)))
    attended_grad = dot_nt(branch, wo_ref[...]).astype(bf16)
    both = dot(mixture, attended_grad)
    put(flat_ref, CROSS.value_weight[0], D, 0, both[:C] + both[C:])
    valued = split(dot_nt(attended_grad, wv_ref[...]), 1)
    delta = column_sum((attended_grad.astype(f32) * attended).T)
    lse = lse_ref[...]
    keyed = split(keyed_ref[...] * LOG2E, 1)
    paired = split(keyed_ref[...], 1)
    gain = vector(vectors_ref, CROSS, CROSS.context_gain)
    bias = vector(vectors_ref, CROSS, CROSS.context_bias)
    acc_ref[...] = jnp.zeros(acc_ref.shape, f32)
    gains_ref[...] = jnp.zeros(gains_ref.shape, f32)
    block = scores_ref.shape[0]

    def visit(index, carry):
        begin = pl.multiple_of(index * block, block)
        some, full = block_kinds(count, begin, block, total)

        @pl.when(some)
        def _():
            unit, rstd = normalise(tokens_ref[pl.ds(begin, block), :].astype(f32))
            context = (unit * gain + bias).astype(bf16)
            twice = jnp.concatenate([context, context], axis=1)
            scores_ref[...] = dot_nt(twice, keyed)

            @pl.when(jnp.logical_not(full))
            def _():
                scores_ref[...] = masked(scores_ref[...], count, begin, total)

            probs = jnp.exp2(scores_ref[...] - lse)
            probs_grad = dot_nt(twice, valued)
            scores_grad = (probs * (probs_grad - delta)).astype(bf16)
            acc_ref[...] += dot_tn(context, scores_grad)
            wide = dot(probs.astype(bf16), valued) + dot(scores_grad, paired)
            context_grad = wide[:, :C] + wide[:, C:]
            gains_ref[0:1, :] += column_sum(context_grad * unit)
            gains_ref[1:2, :] += column_sum(context_grad)
            token_grad_ref[pl.ds(begin, block), :] = normalise_back(context_grad, unit, rstd, gain)

        @pl.when(jnp.logical_not(some))
        def _():
            token_grad_ref[pl.ds(begin, block), :] = jnp.zeros((block, C), f32)

        return carry

    lax.fori_loop(0, total // block, visit, 0)
    put_vector(flat_ref, CROSS.context_gain[0], gains_ref[0:1, :])
    put_vector(flat_ref, CROSS.context_bias[0], gains_ref[1:2, :])
    pulled = split(acc_ref[...] * D ** (-0.5), 0)
    both = dot(pulled, query_ref[...])
    put(flat_ref, CROSS.key_weight[0], D, 0, both[:C] + both[C:])
    query_grad = dot_tn(pulled, jnp.concatenate([wk_ref[...], wk_ref[...]], axis=0)).astype(bf16)
    put(flat_ref, CROSS.query_weight[0], D, 0, dot_tn(normedq_ref[...], query_grad))
    normed_grad = dot_nt(query_grad, wq_ref[...])
    unit, rstd = normalise(start_ref[...])
    put_vector(flat_ref, CROSS.query_gain[0], column_sum(normed_grad * unit))
    put_vector(flat_ref, CROSS.query_bias[0], column_sum(normed_grad))
    start_grad = hidden_grad + normalise_back(normed_grad, unit, rstd, vector(vectors_ref, CROSS, CROSS.query_gain))
    put(flat_ref, CROSS.latents[0], D, 0, start_grad)
    first, unused = CROSS.task_table
    chunks = D // LANES
    flat_ref[first : first + NTASK * chunks, :] = jnp.zeros((NTASK * chunks, LANES), f32)
    sums = column_sum(start_grad)
    base = first + task_ref[0] * chunks
    for chunk in range(chunks):
        flat_ref[pl.ds(base + chunk, 1), :] = sums[:, chunk * LANES : (chunk + 1) * LANES]
    to_windows(flat_ref, windows_ref, windows)


def cross_backward(count, task, tokens, grad, start, vectors, wq, wk, wv, wo, up, down, saved, windows):
    block = min(BLOCK, tokens.shape[0])
    outs = [
        shape(tokens.shape, f32),
        shape((windows.devices * windows.rows, LANES), bf16),
    ]
    scratch = [
        pltpu.VMEM((windows.padded, LANES), f32), pltpu.VMEM((LAT, FF), bf16), pltpu.VMEM((block, LAT), f32),
        pltpu.VMEM((C, LAT), f32), pltpu.VMEM((8, C), f32),
    ]
    return call(
        functools.partial(cross_backward_kernel, windows), "cross_backward", outs,
        [count, task, tokens, grad, start, vectors, wq, wk, wv, wo, up, down, *saved], scratch=scratch,
        smem=2, flops=25_000_000_000, moved=24_000_000,
    )


def body(tokens, task_id, valid_count, cross_params, latent_params, out_grad):
    devices = lax.axis_size(AXES)
    index = lax.axis_index(AXES)
    cross_windows = Windows(cross_params.shape[0] * devices, devices)
    latent_windows = Windows(latent_params.shape[0] * devices, devices)
    cross_all = lax.all_gather(place(cross_params, cross_windows, index), AXES, axis=0, tiled=True)
    latent_all = lax.all_gather(place(latent_params, latent_windows, index), AXES, axis=0, tiled=True)
    vectors, start, wq, wk, wv, wo, up, down = unpack_cross(cross_all, task_id, cross_windows)
    *saved, first = cross_forward(valid_count, tokens[0], start, vectors, wq, wk, wv, wo, up, down)
    latent_weights = unpack_latent(latent_all, latent_windows)
    latents_out, first_grad, latent_grads = latent_layer(first, out_grad[0], *latent_weights, latent_windows)
    latent_window = lax.psum_scatter(latent_grads, AXES, scatter_dimension=0, tiled=True)
    token_grad, cross_grads = cross_backward(
        valid_count, task_id, tokens[0], first_grad, start, vectors, wq, wk, wv, wo, up, down, saved,
        cross_windows,
    )
    cross_window = lax.psum_scatter(cross_grads, AXES, scatter_dimension=0, tiled=True)
    return (
        latents_out[None],
        token_grad[None],
        extract(cross_window, cross_windows, index),
        extract(latent_window, latent_windows, index),
    )


def solution(mesh):
    return jax.shard_map(
        body,
        mesh=mesh,
        in_specs=(
            P(AXES, None, None),
            P(AXES),
            P(AXES),
            P(AXES),
            P(AXES),
            P(AXES, None, None),
        ),
        out_specs=(
            P(AXES, None, None),
            P(AXES, None, None),
            P(AXES),
            P(AXES),
        ),
        check_vma=False,
    )
```

time: 1350 us -> 513 us (0.38); the launches traced: 1320 us -> 507 us
  local copies, waits for them, and re-layouts: 316 us -> 3.24 us
  matrix products: 296 us -> 0 us
  waiting for transfers between devices: 597 us -> 378 us
  Pallas kernels: 0 us -> 110 us
  other arithmetic: 81.5 us -> 0 us
  loops' own time: 16.3 us -> 0 us
    unnamed x4, waiting for transfers between devices: 597 us -> 0.57 us
    dot_general x92 -> x0, matrix products: 296 us -> none  [the longest x26 116 us: product(): return jnp.dot(left, right, preferred_element_type=jnp.float32)]
    reduce_scatter x0 -> x2, waiting for transfers between devices: none -> 266 us  [the longest x1 148 us: body(): lax.psum_scatter(latent_grads, AXES, scatter_dimension=0, tiled=True)]
    unnamed x255 -> x0, local copies, waits for them, and re-layouts: 226 us -> none
    all_gather x0 -> x2, waiting for transfers between devices: none -> 112 us  [the longest x1 68 us: body(): lax.all_gather(place(cross_params, cross_windows, index), AXES, axis=0, t...]
    pallas_call x0 -> x9, Pallas kernels: none -> 110 us  [call(): pl.pallas_call(kernel, name=name, out_shape=outs, in_specs=specs, out_spe...]
    reduce_sum x30 -> x0, other arithmetic: 45.9 us -> none  [the longest x8 17.3 us: accumulate_total(): jnp.sum(shifted, axis=-1)]
    reshape x9 -> x2, local copies, waits for them, and re-layouts: 23.5 us -> 3.24 us  [place(): jnp.pad(shard, (0, rows * LANES - windows.shard)).reshape(rows, LANES)]
  transfers between devices with their start and end apart: 2 -> 4, of which waited for: 2 -> 4; matrix products, arithmetic and copies ran while one was open for 1% -> 0% of each run, Pallas kernels for 0% -> 7%
where the time goes in v1:
time: 513 us; the launch traced here: 507 us
  waiting for transfers between devices  378 us (74%)
  Pallas kernels  110 us (21%)
  between operations  15.5 us (3%)
    reduce_scatter x1, waiting for transfers between devices, body(): lax.psum_scatter(latent_grads, AXES, scatter_dimension=0, tiled=True)  148 us
    reduce_scatter x1, waiting for transfers between devices, body(): lax.psum_scatter(cross_grads, AXES, scatter_dimension=0, tiled=True)  118 us
    pallas_call x9, Pallas kernels, call(): pl.pallas_call(kernel, name=name, out_shape=outs, in_specs=specs, out_spe...  110 us
    all_gather x1, waiting for transfers between devices, body(): lax.all_gather(place(cross_params, cross_windows, index), AXES, axis=0, t...  68 us
    all_gather x1, waiting for transfers between devices, body(): lax.all_gather(place(latent_params, latent_windows, index), AXES, axis=0,...  43.6 us
  transfers between devices with their start and end apart: 4, of which 4 were waited for; matrix products, arithmetic and copies ran while one was open for 0% of the time, Pallas kernels for 7%

profile of v1, /device:TPU:0, one launch (start us, length us, event | category | flops | bytes accessed | tf_op | source)
XLA Modules:
  0.0 506.8 jit_solution(10728518574083871937)
XLA Ops:
  7.2 0.0 all-gather.3.cloned.1.call-start
  7.2 1.6 pad_bitcast_fusion.1.shard_ref
  8.8 1.9 place.2
  10.7 0.0 all-gather.3.cloned.1.call-update
  10.7 0.0 all-gather.5.cloned.1.call-start
  10.8 1.6 pad_bitcast_fusion.shard_ref
  12.4 1.9 place.3
  14.3 0.0 all-gather.5.cloned.1.call-update
  14.4 0.0 reduce-scatter.3.cloned.1.call-start
  15.7 68.0 %all-gather.3.cloned.1.call-done.gathered_ref = bf16[24576,128]{1,0:T(8,128)(2,1)} async-done(((bf16[768,128]{1,0:T(8,128)(2,1)}), bf16[24576,128]{1,0:T(8,128)(2,1)}) %all-gather.3.cloned.1.call-update) | async-done | bytes 6291472 | tf_op jit(solution)/shard_map/all_gather | solution.py:649
  83.7 8.7 %unpack_cross.1 = (f32[16,2048]{1,0:T(8,128)}, f32[512,512]{1,0:T(8,128)}, bf16[512,512]{1,0:T(8,128)(2,1)}, bf16[128,512]{1,0:T(8,128)(2,1)}, bf16[128,512]{1,0...) custom-call(s32[1]{0:T(128)S(6)} %copy.10.task_ref, ...), custom_call_target="tpu_custom_call" | custom-call | tf_op jit(solution)/shard_map/unpack_cross/pallas_call | solution.py:142
  92.4 20.4 %cross_forward.1 = (bf16[512,512]{1,0:T(8,128)(2,1)}, bf16[512,512]{1,0:T(8,128)(2,1)}, f32[512,128]{1,0:T(8,128)}, f32[128,512]{1,0:T(8,128)}, f32[1,512]{1,0:T...) custom-call(s32[1]{0:T(128)S(6)} %copy.11.count_ref, ...), custom_call_target="tpu_custom_call" | custom-call | flops 15000000512 | bytes 16000000 | tf_op jit(solution)/shard_map/cross_forward/pallas_call | solution.py:142
  112.9 43.6 %all-gather.5.cloned.1.call-done.gathered_ref = bf16[25600,128]{1,0:T(8,128)(2,1)} async-done(((bf16[800,128]{1,0:T(8,128)(2,1)}), bf16[25600,128]{1,0:T(8,128)(2,1)}) %all-gather.5.cloned.1.call-update) | async-done | bytes 6553616 | tf_op jit(solution)/shard_map/all_gather | solution.py:650
  156.5 8.8 %unpack_latent.1 = (f32[8,2048]{1,0:T(8,128)}, bf16[512,1536]{1,0:T(8,128)(2,1)}, bf16[512,512]{1,0:T(8,128)(2,1)}, bf16[512,2048]{1,0:T(8,128)(2,1)}, bf16[2048,512]{1,0:T(8,128)(2,1)}) custom-call(bf16[25600,128]{1,0:T(8,128)(2,1)} %all-gather.5.cloned.1.call-done.gathered_ref), custom_call_target="tpu_custom_call" | custom-call | tf_op jit(solution)/shard_map/unpack_latent/pallas_call | solution.py:142
  165.2 28.5 %latent_layer.1 = (bf16[512,512]{1,0:T(8,128)(2,1)}, f32[512,512]{1,0:T(8,128)}, bf16[25600,128]{1,0:T(8,128)(2,1)}) custom-call(f32[512,512]{1,0:T(8,128)} %get-tuple-element.40.hidden_ref, bf16[512,512]{1,0:T(8,128)(2,1)} %bitcast.18, f32[8,2048]{1,0:T(8,128)} %get-tuple-element.41.vectors_ref, bf16[512,1536]{1,0:T(8,128)(2,1)} %get-tuple-element.42.joint_w_ref, ...), custom_call_target="tpu_custom_call" | custom-call | flops 20000000000 | bytes 16000000 | tf_op jit(solution)/shard_map/latent_layer/pallas_call | solution.py:142
  193.7 35.6 %cross_backward.1 = (f32[8192,128]{1,0:T(8,128)}, bf16[24576,128]{1,0:T(8,128)(2,1)}) custom-call(s32[1]{0:T(128)S(6)} %copy.11.count_ref, s32[1]{0:T(128)S(6)} %copy.10.task_ref, bf16[8192,128]{1,0:T(8,128)(2,1)} %bitcast.17, f32[512,512]{1,0:T(8,128)} %get-tuple-element.47.grad_ref, f32[512,512]{1,0:T(8,128)} %get-tuple-element.32.start_ref, ...), custom_call_target="tpu_custom_call" | custom-call | flops 24999999488 | bytes 24000000 | tf_op jit(solution)/shard_map/cross_backward/pallas_call | solution.py:142
  229.4 0.0 reduce-scatter.3.cloned.1.call-update
  229.4 0.0 reduce-scatter.5.cloned.1.call-start
  229.4 0.5 reduce-scatter.5.cloned.1.call-update
  230.0 118.2 %reduce-scatter.3.cloned.1.call-done.window_ref = bf16[768,128]{1,0:T(8,128)(2,1)} async-done(((bf16[24576,128]{1,0:T(8,128)(2,1)}), bf16[768,128]{1,0:T(8,128)(2,1)}) %reduce-scatter.3.cloned.1.call-update) | async-done | bytes 196624 | tf_op jit(solution)/shard_map/reduce_scatter | solution.py:660
  348.2 1.9 extract.2
  350.1 147.8 %reduce-scatter.5.cloned.1.call-done.window_ref = bf16[800,128]{1,0:T(8,128)(2,1)} async-done(((bf16[25600,128]{1,0:T(8,128)(2,1)}), bf16[800,128]{1,0:T(8,128)(2,1)}) %reduce-scatter.5.cloned.1.call-update) | async-done | bytes 204816 | tf_op jit(solution)/shard_map/reduce_scatter | solution.py:655
  497.9 2.0 extract.3
Async XLA Ops:
  7.2 76.6 %all-gather.3.cloned.1.call-start = ((), (), s32[]{:S(2)}) async-start(), calls=%async_computation.2 | async-start | bytes 6488064 | tf_op jit(solution)/shard_map/all_gather | solution.py:649
  10.7 145.7 %all-gather.5.cloned.1.call-start = ((), (), s32[]{:S(2)}) async-start(), calls=%async_computation.3 | async-start | bytes 6758400 | tf_op jit(solution)/shard_map/all_gather | solution.py:650
  14.4 333.8 %reduce-scatter.3.cloned.1.call-start = ((), (), s32[]{:S(2)}) async-start(), calls=%async_computation.4 | async-start | bytes 6488064 | tf_op jit(solution)/shard_map/reduce_scatter | solution.py:660
  229.4 268.5 %reduce-scatter.5.cloned.1.call-start = ((), (), s32[]{:S(2)}) async-start(), calls=%async_computation.5 | async-start | bytes 6758400 | tf_op jit(solution)/shard_map/reduce_scatter | solution.py:655
Sparse Core Ops, SparseCore 0:
  11.6 72.1 all-gather.2
  87.2 69.2 all-gather.4
  229.5 118.6 reduce-scatter.2
  350.4 147.4 reduce-scatter.4
